TPU v7x, 32 devices: a whole 2x2x4 slice. The times are simulated.
32 devices in a mesh: ctx: 16 (over z, x, core), fsdp: 2 (over y).
Axes of the slice: x: 2, y: 2, z: 4, core: 2. Of those that a mesh axis runs over, the one named last changes fastest.
Arguments:
- layer_input: bfloat16 [4096, 2, 768], P('ctx', 'fsdp'), may hold values from -6 to 6
- teacher_states: bfloat16 [4096, 2, 768], P('ctx', 'fsdp'), may hold values from -9 to 9
- seq_lengths: int32 [2], P('fsdp'), may hold values from 1024 to 4096, as said below
- query_weight: bfloat16 [768, 768], P('fsdp'), may hold values from -0.21875 to 0.21875
- query_bias: bfloat16 [768], P('fsdp'), may hold values from -3 to 3
- key_weight: bfloat16 [768, 768], P('fsdp'), may hold values from -0.21875 to 0.21875
- value_weight: bfloat16 [768, 768], P('fsdp'), may hold values from -0.21875 to 0.21875
- value_bias: bfloat16 [768], P('fsdp'), may hold values from -0.119628906 to 0.119628906
- out_weight: bfloat16 [768, 768], P('fsdp'), may hold values from -12 to 12
- out_bias: bfloat16 [768], P('fsdp'), may hold values from -3 to 3
- attn_gain: bfloat16 [768], P('fsdp'), may hold values from 0.5 to 1.5
- attn_shift: bfloat16 [768], P('fsdp'), may hold values from -1.796875 to 1.796875
- inner_weight: bfloat16 [768, 3072], P('fsdp'), may hold values from -0.21875 to 0.21875
- inner_bias: bfloat16 [3072], P('fsdp'), may hold values from -3 to 3
- outer_weight: bfloat16 [3072, 768], P('fsdp'), may hold values from -0.109375 to 0.109375
- outer_bias: bfloat16 [768], P('fsdp'), may hold values from -1.796875 to 1.796875
- final_gain: bfloat16 [768], P('fsdp'), may hold values from 0.5 to 1.5
- final_shift: bfloat16 [768], P('fsdp'), may hold values from -1.796875 to 1.796875
Outputs:
- distill_loss: float32 [], replicated
- layer_output: float32 [4096, 2, 768], P('ctx', 'fsdp')
- input_grad: float32 [4096, 2, 768], P('ctx', 'fsdp')
- query_weight_grad: float32 [768, 768], P('fsdp')
- query_bias_grad: float32 [768], P('fsdp')
- key_weight_grad: float32 [768, 768], P('fsdp')
- value_weight_grad: float32 [768, 768], P('fsdp')
- value_bias_grad: float32 [768], P('fsdp')
- out_weight_grad: float32 [768, 768], P('fsdp')
- out_bias_grad: float32 [768], P('fsdp')
- attn_gain_grad: float32 [768], P('fsdp')
- attn_shift_grad: float32 [768], P('fsdp')
- inner_weight_grad: float32 [768, 3072], P('fsdp')
- inner_bias_grad: float32 [3072], P('fsdp')
- outer_weight_grad: float32 [3072, 768], P('fsdp')
- outer_bias_grad: float32 [768], P('fsdp')
- final_gain_grad: float32 [768], P('fsdp')
- final_shift_grad: float32 [768], P('fsdp')
Inputs may be any that keep to these rules, and one draw needn't show every extreme that they name: `seq_lengths`: at least one of the 2 sequences has all 4096 tokens valid; in each group of 1 sequence on one index of fsdp, one has more than 3840 valid tokens.
All inputs are finite; a program needn't handle non-finite values.
Results may differ from a plain program's by a relative error of at most 0.013.
Values may be sent and summed in bfloat16 or wider, within the bound.
No kernel may reach another device: no remote copies, remote signals or barrier semaphores. Data moves between devices by JAX's collectives and lax.ppermute only.
A program may use at most 192 MiB of HBM per device.

v0:
```python
from functools import partial
import math

import jax
import jax.numpy as jnp
from jax import lax
from jax.sharding import PartitionSpec as P

H = 12


key_block = 512
norm_eps = 1e-12
log_two = math.log(2.0)
masked_score = -1e30


def layer_norm(hidden, norm_gain, norm_shift):
    centre = hidden - jnp.mean(hidden, axis=-1, keepdims=True)
    inverse = lax.rsqrt(jnp.mean(centre * centre, axis=-1, keepdims=True) + norm_eps)
    return centre * inverse * norm_gain + norm_shift


def gelu_exact(hidden_pre):
    return jax.nn.gelu(hidden_pre, approximate=False)


def matmul(left_op, right_op):
    return jnp.dot(left_op, right_op, preferred_element_type=jnp.float32)


def matmul_back(left_op, right_op):
    return lax.dot_general(
        left_op, right_op, (((1,), (1,)), ((), ())), preferred_element_type=jnp.float32
    )


def weight_grad(left_op, right_op):
    return lax.dot_general(
        left_op, right_op, (((0,), (0,)), ((), ())), preferred_element_type=jnp.float32
    )


def split_heads(tensor, head_count):
    return tensor.reshape(
        tensor.shape[0], tensor.shape[1], head_count, tensor.shape[2] // head_count
    )


def score_block(queries, keys_blk, row_start, lengths, head_count):
    head_size = queries.shape[2] // head_count
    raw_scores = jnp.einsum(
        "sghe,kghe->ghsk",
        split_heads(queries, head_count),
        split_heads(keys_blk, head_count),
        preferred_element_type=jnp.float32,
    )
    scaled = raw_scores * (1.0 / (log_two * math.sqrt(head_size)))
    position = row_start + lax.broadcasted_iota(jnp.int32, (1, 1, 1, keys_blk.shape[0]), 3)
    return jnp.where(position < lengths.reshape(-1, 1, 1, 1), scaled, masked_score)


def fold_step(running, shard_pair, row_start, queries, lengths, head_count):
    keys_all, values_all = shard_pair
    row_count = keys_all.shape[0]
    block_rows = math.gcd(row_count, key_block)
    seg_rows, groups, model_width = queries.shape

    def fold_block(states, offset):
        row_top, row_total, accum = states
        keys_blk = lax.dynamic_slice_in_dim(keys_all, offset, block_rows, 0)
        values_blk = lax.dynamic_slice_in_dim(values_all, offset, block_rows, 0)
        scores = score_block(queries, keys_blk, row_start + offset, lengths, head_count)
        new_top = jnp.maximum(row_top, jnp.floor(jnp.max(scores, axis=-1)))
        factor = jnp.exp2(row_top - new_top)
        exp_weights = jnp.exp2(scores - new_top[..., None])
        row_total = row_total * factor + jnp.sum(exp_weights, axis=-1)
        partial_sum = jnp.einsum(
            "ghsk,kghe->sghe",
            exp_weights.astype(jnp.bfloat16),
            split_heads(values_blk, head_count),
            preferred_element_type=jnp.float32,
        )
        rescaled = (
            split_heads(accum, head_count) * jnp.transpose(factor, (2, 0, 1))[..., None]
            + partial_sum
        )
        return ((new_top, row_total, rescaled.reshape(seg_rows, groups, model_width)), None)

    offsets = jnp.arange(row_count // block_rows, dtype=jnp.int32) * block_rows
    running, _ = lax.scan(fold_block, running, offsets)
    return running


def block_signals(keys_blk, values_blk, row_start, saved_state, head_count):
    queries, lengths, row_top, grad_numer, delta_rows = saved_state
    scores = score_block(queries, keys_blk, row_start, lengths, head_count)
    exp_weights = jnp.exp2(scores - row_top[..., None])
    along_values = jnp.einsum(
        "sghe,kghe->ghsk",
        split_heads(grad_numer, head_count),
        split_heads(values_blk, head_count),
        preferred_element_type=jnp.float32,
    )
    grad_scores = (log_two * exp_weights * (along_values - delta_rows[..., None])).astype(
        jnp.bfloat16
    )
    return (exp_weights.astype(jnp.bfloat16), grad_scores)


def key_side(weights_low, grad_scores, saved_state, head_count, score_scale):
    queries, grad_numer = (saved_state[0], saved_state[3])
    block_rows = weights_low.shape[3]
    grad_key = (
        jnp.einsum(
            "ghsk,sghe->kghe",
            grad_scores,
            split_heads(queries, head_count),
            preferred_element_type=jnp.float32,
        )
        * score_scale
    )
    grad_value = jnp.einsum(
        "ghsk,sghe->kghe",
        weights_low,
        split_heads(grad_numer, head_count),
        preferred_element_type=jnp.float32,
    )
    return (
        grad_key.reshape(block_rows, queries.shape[1], queries.shape[2]),
        grad_value.reshape(block_rows, queries.shape[1], queries.shape[2]),
    )


def query_part(grad_scores, keys_blk, head_count, score_scale):
    part_rows = (
        jnp.einsum(
            "ghsk,kghe->sghe",
            grad_scores,
            split_heads(keys_blk, head_count),
            preferred_element_type=jnp.float32,
        )
        * score_scale
    )
    return part_rows.reshape(part_rows.shape[0], part_rows.shape[1], keys_blk.shape[2])


def shards(
    layer_input,
    teacher_states,
    seq_lengths,
    query_weight,
    query_bias,
    key_weight,
    value_weight,
    value_bias,
    out_weight,
    out_bias,
    attn_gain,
    attn_shift,
    inner_weight,
    inner_bias,
    outer_weight,
    outer_bias,
    final_gain,
    final_shift,
):
    seg_rows, groups, model_width = layer_input.shape
    head_count = H
    score_scale = 1.0 / (log_two * math.sqrt(model_width // head_count))
    (
        w_query,
        b_query,
        w_key,
        w_value,
        b_value,
        w_out,
        b_out,
        g_attn,
        s_attn,
        w_inner,
        b_inner,
        w_outer,
        b_outer,
        g_final,
        s_final,
    ) = (
        lax.all_gather(query_weight, "fsdp", axis=0, tiled=True),
        lax.all_gather(query_bias, "fsdp", axis=0, tiled=True),
        lax.all_gather(key_weight, "fsdp", axis=0, tiled=True),
        lax.all_gather(value_weight, "fsdp", axis=0, tiled=True),
        lax.all_gather(value_bias, "fsdp", axis=0, tiled=True),
        lax.all_gather(out_weight, "fsdp", axis=0, tiled=True),
        lax.all_gather(out_bias, "fsdp", axis=0, tiled=True),
        lax.all_gather(attn_gain, "fsdp", axis=0, tiled=True),
        lax.all_gather(attn_shift, "fsdp", axis=0, tiled=True),
        lax.all_gather(inner_weight, "fsdp", axis=0, tiled=True),
        lax.all_gather(inner_bias, "fsdp", axis=0, tiled=True),
        lax.all_gather(outer_weight, "fsdp", axis=0, tiled=True),
        lax.all_gather(outer_bias, "fsdp", axis=0, tiled=True),
        lax.all_gather(final_gain, "fsdp", axis=0, tiled=True),
        lax.all_gather(final_shift, "fsdp", axis=0, tiled=True),
    )
    b_query = b_query.astype(jnp.float32)
    b_value = b_value.astype(jnp.float32)
    b_out = b_out.astype(jnp.float32)
    g_attn = g_attn.astype(jnp.float32)
    s_attn = s_attn.astype(jnp.float32)
    b_inner = b_inner.astype(jnp.float32)
    b_outer = b_outer.astype(jnp.float32)
    g_final = g_final.astype(jnp.float32)
    s_final = s_final.astype(jnp.float32)
    token_rows = layer_input.reshape(seg_rows * groups, model_width)
    queries = (
        (matmul(token_rows, w_query) + b_query)
        .astype(jnp.bfloat16)
        .reshape(seg_rows, groups, model_width)
    )
    key_proj = matmul(token_rows, w_key).astype(jnp.bfloat16).reshape(seg_rows, groups, model_width)
    value_proj = (
        (matmul(token_rows, w_value) + b_value)
        .astype(jnp.bfloat16)
        .reshape(seg_rows, groups, model_width)
    )
    initial = (
        jnp.full((groups, head_count, seg_rows), masked_score, jnp.float32),
        jnp.zeros((groups, head_count, seg_rows), jnp.float32),
        jnp.zeros((seg_rows, groups, model_width), jnp.float32),
    )
    folder = partial(fold_step, queries=queries, lengths=seq_lengths, head_count=head_count)
    key_full, value_full = (
        lax.all_gather(key_proj, "ctx", axis=0, tiled=True),
        lax.all_gather(value_proj, "ctx", axis=0, tiled=True),
    )
    row_top, row_total, accum = folder(initial, (key_full, value_full), 0)
    per_head = jnp.transpose(row_total, (2, 0, 1))[..., None]
    context = split_heads(accum, head_count) / per_head
    context_low = context.reshape(seg_rows * groups, model_width).astype(jnp.bfloat16)
    attn_out = matmul(context_low, w_out) + b_out
    pre_norm = token_rows.astype(jnp.float32) + attn_out
    normed = layer_norm(pre_norm, g_attn, s_attn)
    normed_low = normed.astype(jnp.bfloat16)
    hidden_pre = matmul(normed_low, w_inner) + b_inner
    act_low = gelu_exact(hidden_pre).astype(jnp.bfloat16)
    branch = matmul(act_low, w_outer) + b_outer
    pre_final = normed + branch
    output = layer_norm(pre_final, g_final, s_final)
    target = teacher_states.reshape(seg_rows * groups, model_width).astype(jnp.float32)
    position = lax.axis_index("ctx") * seg_rows + lax.broadcasted_iota(
        jnp.int32, (seg_rows, groups), 0
    )
    valid_mask = (position < seq_lengths.reshape(1, groups)).astype(jnp.float32)
    mismatch = output - target
    total_sq, valid_count = lax.psum(
        (jnp.sum(valid_mask * mismatch * mismatch), jnp.sum(valid_mask)), ("ctx", "fsdp")
    )
    distill_loss = total_sq / (model_width * valid_count)
    token_total = seg_rows * groups * lax.axis_size("ctx") * lax.axis_size("fsdp")
    grad_out = 2.0 * valid_mask * mismatch * (token_total / valid_count)
    _, final_pull = jax.vjp(layer_norm, pre_final, g_final, s_final)
    grad_mid, final_gain_grad, final_shift_grad = final_pull(grad_out)
    grad_branch = grad_mid.astype(jnp.bfloat16)
    outer_bias_grad = jnp.sum(grad_branch, axis=0, dtype=jnp.float32)
    outer_weight_grad = weight_grad(act_low, grad_branch)
    _, gelu_pull = jax.vjp(gelu_exact, hidden_pre)
    grad_hidden = gelu_pull(matmul_back(grad_branch, w_outer))[0].astype(jnp.bfloat16)
    inner_bias_grad = jnp.sum(grad_hidden, axis=0, dtype=jnp.float32)
    inner_weight_grad = weight_grad(normed_low, grad_hidden)
    grad_normed = grad_mid + matmul_back(grad_hidden, w_inner)
    _, attn_pull = jax.vjp(layer_norm, pre_norm, g_attn, s_attn)
    grad_sum, attn_gain_grad, attn_shift_grad = attn_pull(grad_normed)
    grad_attn = grad_sum.astype(jnp.bfloat16)
    out_bias_grad = jnp.sum(grad_attn, axis=0, dtype=jnp.float32)
    out_weight_grad = weight_grad(context_low, grad_attn)
    grad_context = (
        matmul_back(grad_attn, w_out).astype(jnp.bfloat16).reshape(seg_rows, groups, model_width)
    )
    context_wide = split_heads(grad_context, head_count).astype(jnp.float32)
    grad_numer = (
        (context_wide / per_head).astype(jnp.bfloat16).reshape(seg_rows, groups, model_width)
    )
    delta_rows = jnp.transpose(
        jnp.sum(context_wide * context, axis=-1) / per_head[..., 0], (1, 2, 0)
    )
    saved_state = (queries, seq_lengths, row_top, grad_numer, delta_rows)
    key_value = (key_full, value_full)
    length = key_value[0].shape[0]
    block_rows = math.gcd(length, key_block)
    offsets = jnp.arange(length // block_rows, dtype=jnp.int32) * block_rows
    zero_rows = jnp.zeros((seg_rows, groups, model_width), jnp.float32)

    def whole_block(grad_query, offset):
        keys_blk = lax.dynamic_slice_in_dim(key_value[0], offset, block_rows, 0)
        values_blk = lax.dynamic_slice_in_dim(key_value[1], offset, block_rows, 0)
        weights_low, grad_scores = block_signals(
            keys_blk, values_blk, offset, saved_state, head_count
        )
        grad_query = grad_query + query_part(grad_scores, keys_blk, head_count, score_scale)
        return (
            grad_query,
            key_side(weights_low, grad_scores, saved_state, head_count, score_scale),
        )

    grad_query, (key_parts, value_parts) = lax.scan(whole_block, zero_rows, offsets)
    grad_keys, grad_values = (
        lax.psum_scatter(
            key_parts.reshape(length, groups, model_width), "ctx", scatter_dimension=0, tiled=True
        ),
        lax.psum_scatter(
            value_parts.reshape(length, groups, model_width), "ctx", scatter_dimension=0, tiled=True
        ),
    )
    query_rows = grad_query.astype(jnp.bfloat16).reshape(seg_rows * groups, model_width)
    key_rows_low = grad_keys.astype(jnp.bfloat16).reshape(seg_rows * groups, model_width)
    value_rows = grad_values.astype(jnp.bfloat16).reshape(seg_rows * groups, model_width)
    query_weight_grad = weight_grad(token_rows, query_rows)
    query_bias_grad = jnp.sum(query_rows, axis=0, dtype=jnp.float32)
    key_weight_grad = weight_grad(token_rows, key_rows_low)
    value_weight_grad = weight_grad(token_rows, value_rows)
    value_bias_grad = jnp.sum(value_rows, axis=0, dtype=jnp.float32)
    input_grad = (
        grad_sum
        + matmul_back(query_rows, w_query)
        + matmul_back(key_rows_low, w_key)
        + matmul_back(value_rows, w_value)
    )
    (
        query_weight_grad,
        query_bias_grad,
        key_weight_grad,
        value_weight_grad,
        value_bias_grad,
        out_weight_grad,
        out_bias_grad,
        attn_gain_grad,
        attn_shift_grad,
        inner_weight_grad,
        inner_bias_grad,
        outer_weight_grad,
        outer_bias_grad,
        final_gain_grad,
        final_shift_grad,
    ) = (
        lax.psum_scatter(query_weight_grad, "fsdp", scatter_dimension=0, tiled=True),
        lax.psum_scatter(query_bias_grad, "fsdp", scatter_dimension=0, tiled=True),
        lax.psum_scatter(key_weight_grad, "fsdp", scatter_dimension=0, tiled=True),
        lax.psum_scatter(value_weight_grad, "fsdp", scatter_dimension=0, tiled=True),
        lax.psum_scatter(value_bias_grad, "fsdp", scatter_dimension=0, tiled=True),
        lax.psum_scatter(out_weight_grad, "fsdp", scatter_dimension=0, tiled=True),
        lax.psum_scatter(out_bias_grad, "fsdp", scatter_dimension=0, tiled=True),
        lax.psum_scatter(attn_gain_grad, "fsdp", scatter_dimension=0, tiled=True),
        lax.psum_scatter(attn_shift_grad, "fsdp", scatter_dimension=0, tiled=True),
        lax.psum_scatter(inner_weight_grad, "fsdp", scatter_dimension=0, tiled=True),
        lax.psum_scatter(inner_bias_grad, "fsdp", scatter_dimension=0, tiled=True),
        lax.psum_scatter(outer_weight_grad, "fsdp", scatter_dimension=0, tiled=True),
        lax.psum_scatter(outer_bias_grad, "fsdp", scatter_dimension=0, tiled=True),
        lax.psum_scatter(final_gain_grad, "fsdp", scatter_dimension=0, tiled=True),
        lax.psum_scatter(final_shift_grad, "fsdp", scatter_dimension=0, tiled=True),
    )
    (
        query_weight_grad,
        query_bias_grad,
        key_weight_grad,
        value_weight_grad,
        value_bias_grad,
        out_weight_grad,
        out_bias_grad,
        attn_gain_grad,
        attn_shift_grad,
        inner_weight_grad,
        inner_bias_grad,
        outer_weight_grad,
        outer_bias_grad,
        final_gain_grad,
        final_shift_grad,
    ) = lax.psum(
        (
            query_weight_grad,
            query_bias_grad,
            key_weight_grad,
            value_weight_grad,
            value_bias_grad,
            out_weight_grad,
            out_bias_grad,
            attn_gain_grad,
            attn_shift_grad,
            inner_weight_grad,
            inner_bias_grad,
            outer_weight_grad,
            outer_bias_grad,
            final_gain_grad,
            final_shift_grad,
        ),
        "ctx",
    )
    return (
        distill_loss,
        output.reshape(seg_rows, groups, model_width),
        input_grad.reshape(seg_rows, groups, model_width),
        query_weight_grad,
        query_bias_grad,
        key_weight_grad,
        value_weight_grad,
        value_bias_grad,
        out_weight_grad,
        out_bias_grad,
        attn_gain_grad,
        attn_shift_grad,
        inner_weight_grad,
        inner_bias_grad,
        outer_weight_grad,
        outer_bias_grad,
        final_gain_grad,
        final_shift_grad,
    )


def solution(mesh):
    placed = (
        P("ctx", "fsdp", None),
        P("ctx", "fsdp", None),
        P("fsdp"),
        P("fsdp", None),
        P("fsdp"),
        P("fsdp", None),
        P("fsdp", None),
        P("fsdp"),
        P("fsdp", None),
        P("fsdp"),
        P("fsdp"),
        P("fsdp"),
        P("fsdp", None),
        P("fsdp"),
        P("fsdp", None),
        P("fsdp"),
        P("fsdp"),
        P("fsdp"),
    )
    return jax.shard_map(
        shards,
        mesh=mesh,
        in_specs=placed,
        out_specs=(
            P(),
            P("ctx", "fsdp", None),
            P("ctx", "fsdp", None),
            P("fsdp", None),
            P("fsdp"),
            P("fsdp", None),
            P("fsdp", None),
            P("fsdp"),
            P("fsdp", None),
            P("fsdp"),
            P("fsdp"),
            P("fsdp"),
            P("fsdp", None),
            P("fsdp"),
            P("fsdp", None),
            P("fsdp"),
            P("fsdp"),
            P("fsdp"),
        ),
        check_vma=False,
    )
```

profile of v0, /device:TPU:0, one launch (start us, length us, event | category | flops | bytes accessed | tf_op | source)
XLA Modules:
  0.0 1581.9 jit_solution(6112549357144248874)
XLA Ops:
  9.5 25.6 %all-gather.20.cloned.1.call-done = bf16[768,768]{1,0:T(8,128)(2,1)} async-done(((bf16[384,768]{1,0:T(8,128)(2,1)}), bf16[768,768]{1,0:T(8,128)(2,1)}) %all-gather.20.cloned.1.call-update) | async-done | bytes 1179664 | tf_op jit(solution)/shard_map/all_gather | solution.py:190
  42.2 17.3 %all-gather.24.cloned.1.call-done = bf16[768,768]{1,0:T(8,128)(2,1)} async-done(((bf16[384,768]{1,0:T(8,128)(2,1)}), bf16[768,768]{1,0:T(8,128)(2,1)}) %all-gather.24.cloned.1.call-update) | async-done | bytes 1179664 | tf_op jit(solution)/shard_map/all_gather | solution.py:191
  66.0 40.0 %psum.120 = f32[]{:T(128)} all-reduce(f32[]{:T(128)} %fusion.57), channel_id=1, replica_groups=mesh['ctx'=16,'fsdp'=2] {'ctx','fsdp'}, use_global_device_ids=true, to_apply=%region_11.12 | all-reduce | flops 1 | bytes 8 | tf_op jit(solution)/shard_map/psum | solution.py:254
  148.9 8.6 copy.81
  157.6 54.6 %all-gather.34.cloned.1.call-done = bf16[4096,768]{1,0:T(8,128)(2,1)} async-done(((bf16[256,768]{1,0:T(8,128)(2,1)}), bf16[4096,768]{1,0:T(8,128)(2,1)}) %all-gather.34.cloned.1.call-update) | async-done | bytes 6291472 | tf_op jit(solution)/shard_map/all_gather | solution.py:233
  212.2 8.7 copy.83
  220.9 139.7 %while.30 = (s32[]{:T(128)}, f32[1,12,256]{2,1,0:T(8,128)S(1)}, f32[1,12,256]{2,1,0:T(8,128)S(1)}, f32[256,1,768]{0,2,1:T(8,128)S(1)}, s32[8]{0:T(128)}, /*index...) while((s32[]{:T(128)}, f32[1,12,256]{2,1,0:T(8,128)S(1)}, ...), condition=%wide.region_3.4_spmd.clone, body=%wide.region_0.3_spmd.clone.sunk | while | flops 423522304 | bytes 50923740 | solution.py:91
  363.0 11.7 multiply_convert_fusion.1
  392.3 254.6 %while.31 = (s32[]{:T(128)}, f32[256,1,768]{0,2,1:T(8,128)}, f32[8,512,1,768]{3,1,0,2:T(8,128)}, f32[8,512,1,768]{3,1,0,2:T(8,128)}, s32[8]{0:T(128)}, /*index=5...) while((s32[]{:T(128)}, f32[256,1,768]{0,2,1:T(8,128)}, ...), condition=%wide.region_18.19_spmd.clone, body=%wide.region_17.18_spmd.clone.sunk | while | flops 1028064256 | bytes 87334736 | solution.py:304
  409.2 5.8 fusion.146
  441.1 5.8 fusion.146
  472.9 5.8 fusion.146
  504.8 5.8 fusion.146
  536.6 5.8 fusion.146
  568.4 5.8 fusion.146
  600.4 5.8 fusion.146
  632.0 5.8 fusion.146
  653.5 6.1 fusion.66
  661.5 6.0 fusion.76
  667.6 113.4 %reduce-scatter.9.cloned.1.call-done = f32[256,1,768]{2,0,1:T(8,128)} async-done(((f32[4096,1,768]{2,0,1:T(8,128)}), f32[256,1,768]{2,0,1:T(8,128)}) %reduce-scatter.9.cloned.1.call-update) | async-done | bytes 786448 | tf_op jit(solution)/shard_map/reduce_scatter | solution.py:306
  784.1 134.7 %reduce-scatter.11.cloned.1.call-done = f32[256,1,768]{2,0,1:T(8,128)} async-done(((f32[4096,1,768]{2,0,1:T(8,128)}), f32[256,1,768]{2,0,1:T(8,128)}) %reduce-scatter.11.cloned.1.call-update) | async-done | bytes 786448 | tf_op jit(solution)/shard_map/reduce_scatter | solution.py:309
  922.2 33.3 %reduce-scatter.13.cloned.1.call-done = f32[384,768]{0,1:T(8,128)} async-done(((f32[768,768]{0,1:T(8,128)}), f32[384,768]{0,1:T(8,128)}) %reduce-scatter.13.cloned.1.call-update) | async-done | bytes 1179664 | tf_op jit(solution)/shard_map/reduce_scatter | solution.py:344
  955.5 36.9 %reduce-scatter.19.cloned.1.call-done = f32[384,768]{1,0:T(8,128)} async-done(((f32[768,768]{1,0:T(8,128)}), f32[384,768]{1,0:T(8,128)}) %reduce-scatter.19.cloned.1.call-update) | async-done | bytes 1179664 | tf_op jit(solution)/shard_map/reduce_scatter | solution.py:349
  992.4 112.9 %reduce-scatter.21.cloned.1.call-done = f32[384,3072]{1,0:T(8,128)} async-done(((f32[768,3072]{1,0:T(8,128)}), f32[384,3072]{1,0:T(8,128)}) %reduce-scatter.21.cloned.1.call-update) | async-done | bytes 4718608 | tf_op jit(solution)/shard_map/reduce_scatter | solution.py:353
  1105.3 112.7 %reduce-scatter.23.cloned.1.call-done = f32[1536,768]{1,0:T(8,128)} async-done(((f32[3072,768]{1,0:T(8,128)}), f32[1536,768]{1,0:T(8,128)}) %reduce-scatter.23.cloned.1.call-update) | async-done | bytes 4718608 | tf_op jit(solution)/shard_map/reduce_scatter | solution.py:355
  1218.0 37.4 %reduce-scatter.15.cloned.1.call-done = f32[384,768]{0,1:T(8,128)} async-done(((f32[768,768]{0,1:T(8,128)}), f32[384,768]{0,1:T(8,128)}) %reduce-scatter.15.cloned.1.call-update) | async-done | bytes 1179664 | tf_op jit(solution)/shard_map/reduce_scatter | solution.py:346
  1255.4 36.9 %reduce-scatter.17.cloned.1.call-done = f32[384,768]{0,1:T(8,128)} async-done(((f32[768,768]{0,1:T(8,128)}), f32[384,768]{0,1:T(8,128)}) %reduce-scatter.17.cloned.1.call-update) | async-done | bytes 1179664 | tf_op jit(solution)/shard_map/reduce_scatter | solution.py:347
  1295.1 41.3 %psum.119 = f32[]{:T(128)} all-reduce(f32[]{:T(128)} %get-tuple-element.367), channel_id=1, replica_groups=mesh['ctx'=16,'fsdp'=2] {'ctx','fsdp'}, use_global_device_ids=true, to_apply=%region_9.10 | all-reduce | flops 1 | bytes 8 | tf_op jit(solution)/shard_map/psum | solution.py:254
  1345.1 9.8 all-reduce.11
  1355.6 60.7 %all-reduce.9 = (f32[384]{0:T(512)}, f32[384]{0:T(512)}, f32[384]{0:T(512)}, f32[384]{0:T(512)}, f32[384]{0:T(512)}, /*index=5*/f32[1536]{0:T(1024)}, f32[384]{0:T(512)}, f32[384]{0:T(512)}, f32[384]{0:T(512)}) all-reduce(f32[384]{0:T(512)S(1)} %dynamic-slice.1, ...), channel_id=1, replica_groups=mesh['ctx'=16,'fsdp'=2] {'ctx'}, use_global_device_ids=true, to_apply=%region_25.26 | all-reduce | flops 4608 | bytes 36864 | tf_op jit(solution)/shard_map/psum | solution.py:376
  1416.3 143.1 %all-reduce.14.cloned.1.call-done = (f32[384,768]{0,1:T(8,128)}, f32[384,768]{0,1:T(8,128)}, f32[384,768]{0,1:T(8,128)}, f32[384,768]{1,0:T(8,128)}, f32[384,3072]{1,0:T(8,128)}, /*index=5*/f32[1536,768]{1,0:T(8,128)}) async-done(((f32[384,768]{0,1:T(8,128)}, f32[384,768]{0,1:T(8,128)}, f32[384,768]{0,1:T(8,128)}, f32[384,768]{1,0:T(8,128)}, f32[384,3072]{1,0:T(8,128)}, /*index=5*/f32[1536,768]{1,0:T(8,128)}), ...) | async-done | bytes 14155792 | tf_op jit(solution)/shard_map/psum | solution.py:376
  1566.0 5.7 copy.158
  (509 shorter events, 424.9 us)
Async XLA Ops:
  7.2 52.3 %copy-start.6 = (bf16[256,1,768]{2,0,1:T(8,128)(2,1)S(1)}, bf16[256,1,768]{2,0,1:T(8,128)(2,1)}, u32[]{:S(2)}) copy-start(bf16[256,1,768]{2,0,1:T(8,128)(2,1)} %param.22) | copy-start | bytes 1179652
  7.2 27.9 %all-gather.20.cloned.1.call-start = ((), (), s32[]{:S(2)}) async-start(), calls=%async_computation.8 | async-start | bytes 1769472 | tf_op jit(solution)/shard_map/all_gather | solution.py:190
  7.9 51.5 %all-gather.24.cloned.1.call-start = ((), (), s32[]{:S(2)}) async-start(), calls=%async_computation.10 | async-start | bytes 1769472 | tf_op jit(solution)/shard_map/all_gather | solution.py:191
  8.7 134.0 %all-gather.22.cloned.1.call-start = ((), (), s32[]{:S(2)}) async-start(), calls=%async_computation.9 | async-start | bytes 1769472 | tf_op jit(solution)/shard_map/all_gather | solution.py:188
  9.4 139.5 %all-gather.32.cloned.1.call-start = ((), (), s32[]{:S(2)}) async-start(), calls=%async_computation.22 | async-start | bytes 6684672 | tf_op jit(solution)/shard_map/all_gather | solution.py:232
  37.8 174.5 %all-gather.34.cloned.1.call-start = ((), (), s32[]{:S(2)}) async-start(), calls=%async_computation.23 | async-start | bytes 6684672 | tf_op jit(solution)/shard_map/all_gather | solution.py:233
  62.0 44.0 %copy-start.48 = (bf16[384]{0:T(512)(128)(2,1)S(1)}, bf16[384]{0:T(512)(128)(2,1)}, u32[]{:S(2)}) copy-start(bf16[384]{0:T(512)(128)(2,1)} %param.39) | copy-start | bytes 2308
  62.0 48.8 %copy-start.49 = (bf16[384]{0:T(512)(128)(2,1)S(1)}, bf16[384]{0:T(512)(128)(2,1)}, u32[]{:S(2)}) copy-start(bf16[384]{0:T(512)(128)(2,1)} %param.38) | copy-start | bytes 2308
  62.0 53.2 %copy-start.50 = (bf16[384]{0:T(512)(128)(2,1)S(1)}, bf16[384]{0:T(512)(128)(2,1)}, u32[]{:S(2)}) copy-start(bf16[384]{0:T(512)(128)(2,1)} %param.37) | copy-start | bytes 2308
  62.0 57.5 %copy-start.44 = (bf16[1536]{0:T(1024)(128)(2,1)S(1)}, bf16[1536]{0:T(1024)(128)(2,1)}, u32[]{:S(2)}) copy-start(bf16[1536]{0:T(1024)(128)(2,1)} %param.35) | copy-start | bytes 9220
  62.0 61.9 %copy-start.51 = (bf16[384]{0:T(512)(128)(2,1)S(1)}, bf16[384]{0:T(512)(128)(2,1)}, u32[]{:S(2)}) copy-start(bf16[384]{0:T(512)(128)(2,1)} %param.31) | copy-start | bytes 2308
  62.0 66.3 %copy-start.52 = (bf16[384]{0:T(512)(128)(2,1)S(1)}, bf16[384]{0:T(512)(128)(2,1)}, u32[]{:S(2)}) copy-start(bf16[384]{0:T(512)(128)(2,1)} %param.26) | copy-start | bytes 2308
  62.0 70.7 %copy-start.53 = (bf16[384]{0:T(512)(128)(2,1)S(1)}, bf16[384]{0:T(512)(128)(2,1)}, u32[]{:S(2)}) copy-start(bf16[384]{0:T(512)(128)(2,1)} %param.33) | copy-start | bytes 2308
  62.0 75.1 %copy-start.54 = (bf16[384]{0:T(512)(128)(2,1)S(1)}, bf16[384]{0:T(512)(128)(2,1)}, u32[]{:S(2)}) copy-start(bf16[384]{0:T(512)(128)(2,1)} %param.32) | copy-start | bytes 2308
  62.0 298.7 %all-gather.26.cloned.1.call-start = ((), (), s32[]{:S(2)}) async-start(), calls=%async_computation.11 | async-start | bytes 1769472 | tf_op jit(solution)/shard_map/all_gather | solution.py:193
  62.6 300.4 %all-gather.28.cloned.1.call-start = ((), (), s32[]{:S(2)}) async-start(), calls=%async_computation.12 | async-start | bytes 7077888 | tf_op jit(solution)/shard_map/all_gather | solution.py:197
  63.4 311.4 %all-gather.30.cloned.1.call-start = ((), (), s32[]{:S(2)}) async-start(), calls=%async_computation.13 | async-start | bytes 7077888 | tf_op jit(solution)/shard_map/all_gather | solution.py:199
  64.1 716.8 %reduce-scatter.9.cloned.1.call-start = ((), (), s32[]{:S(2)}) async-start(), calls=%async_computation.14 | async-start | bytes 13369344 | tf_op jit(solution)/shard_map/reduce_scatter | solution.py:306
  137.1 237.7 %copy-start.31 = (f32[768]{0:T(1024)}, f32[768]{0:T(1024)S(1)}, u32[]{:S(2)}) copy-start(f32[768]{0:T(1024)S(1)} %reshape.401) | copy-start | bytes 9220
  142.0 246.0 %copy-start.29 = (f32[768]{0:T(1024)}, f32[768]{0:T(1024)S(1)}, u32[]{:S(2)}) copy-start(f32[768]{0:T(1024)S(1)} %reshape.400) | copy-start | bytes 9220
  646.9 271.9 %reduce-scatter.11.cloned.1.call-start = ((), (), s32[]{:S(2)}) async-start(), calls=%async_computation.15 | async-start | bytes 13369344 | tf_op jit(solution)/shard_map/reduce_scatter | solution.py:309
  647.5 308.0 %reduce-scatter.13.cloned.1.call-start = ((), (), s32[]{:S(2)}) async-start(), calls=%async_computation.16 | async-start | bytes 3538944 | tf_op jit(solution)/shard_map/reduce_scatter | solution.py:344
  650.2 342.3 %reduce-scatter.19.cloned.1.call-start = ((), (), s32[]{:S(2)}) async-start(), calls=%async_computation.19 | async-start | bytes 3538944 | tf_op jit(solution)/shard_map/reduce_scatter | solution.py:349
  652.1 453.2 %reduce-scatter.21.cloned.1.call-start = ((), (), s32[]{:S(2)}) async-start(), calls=%async_computation.20 | async-start | bytes 14155776 | tf_op jit(solution)/shard_map/reduce_scatter | solution.py:353
  659.7 558.3 %reduce-scatter.23.cloned.1.call-start = ((), (), s32[]{:S(2)}) async-start(), calls=%async_computation.21 | async-start | bytes 14155776 | tf_op jit(solution)/shard_map/reduce_scatter | solution.py:355
  667.5 587.9 %reduce-scatter.15.cloned.1.call-start = ((), (), s32[]{:S(2)}) async-start(), calls=%async_computation.17 | async-start | bytes 3538944 | tf_op jit(solution)/shard_map/reduce_scatter | solution.py:346
  784.0 508.4 %reduce-scatter.17.cloned.1.call-start = ((), (), s32[]{:S(2)}) async-start(), calls=%async_computation.18 | async-start | bytes 3538944 | tf_op jit(solution)/shard_map/reduce_scatter | solution.py:347
  921.9 637.5 %all-reduce.14.cloned.1.call-start = ((), (), s32[]{:S(2)}) async-start(), calls=%async_computation.24 | async-start | bytes 28311552 | tf_op jit(solution)/shard_map/psum | solution.py:376
  1292.4 47.7 %copy-start.10 = (f32[256,768]{1,0:T(8,128)S(1)}, f32[256,768]{1,0:T(8,128)}, u32[]{:S(2)}) copy-start(f32[256,768]{1,0:T(8,128)} %copy-done.9) | copy-start | bytes 2359300
  1292.4 47.7 %copy-start.43 = (f32[256]{0:T(256)S(1)}, f32[256]{0:T(256)}, u32[]{:S(2)}) copy-start(f32[256]{0:T(256)} %copy-done.42) | copy-start | bytes 3076
  1292.4 49.7 %copy-start.11 = (bf16[768,768]{1,0:T(8,128)(2,1)S(1)}, bf16[768,768]{1,0:T(8,128)(2,1)}, u32[]{:S(2)}) copy-start(bf16[768,768]{1,0:T(8,128)(2,1)} %all-gather.20.cloned.1.call-done) | copy-start | bytes 3538948
  1292.4 49.7 %copy-start.17 = (f32[256,1,768]{2,0,1:T(8,128)S(1)}, f32[256,1,768]{2,0,1:T(8,128)}, u32[]{:S(2)}) copy-start(f32[256,1,768]{2,0,1:T(8,128)} %reduce-scatter.9.cloned.1.call-done) | copy-start | bytes 2359300
  (85 other events, 438.9 us)
Sparse Core Ops, SparseCore 0:
  9.6 25.4 all-gather.19
  36.6 22.7 all-gather.23
  61.0 23.4 all-gather.21
  87.2 61.6 all-gather.31
  151.6 60.5 all-gather.33
  213.6 21.3 all-gather.25
  236.6 62.6 all-gather.27
  300.8 62.6 all-gather.29
  647.0 133.8 reduce-scatter.8
  784.8 133.9 reduce-scatter.10
  921.6 33.8 reduce-scatter.12
  957.7 34.6 reduce-scatter.18
  994.7 110.5 reduce-scatter.20
  1107.5 110.5 reduce-scatter.22
  1220.7 34.7 reduce-scatter.14
  1257.6 34.6 reduce-scatter.16
  1297.4 262.0 all-reduce.13
where the time goes:
time: 1590 us; the launch traced here: 1580 us
  waiting for transfers between devices  868 us (55%)
  matrix products  217 us (14%)
  blocking collectives  192 us (12%)
  local copies, waits for them, and re-layouts  167 us (11%)
  other arithmetic  84.6 us (5%)
  loops' own time  32.7 us (2%)
  between operations  20.5 us (1%)
    psum x1, waiting for transfers between devices, shards(): lax.psum((query_weight_grad, query_bias_grad, key_weight_grad, value_weig...  143 us
    reduce_scatter x1, waiting for transfers between devices, shards(): lax.psum_scatter(value_parts.reshape(length, groups, model_width), 'ctx',...  135 us
    reduce_scatter x1, waiting for transfers between devices, shards(): lax.psum_scatter(key_parts.reshape(length, groups, model_width), 'ctx', s...  113 us
    reduce_scatter x1, waiting for transfers between devices, shards(): lax.psum_scatter(inner_weight_grad, 'fsdp', scatter_dimension=0, tiled=True)  113 us
    reduce_scatter x1, waiting for transfers between devices, shards(): lax.psum_scatter(outer_weight_grad, 'fsdp', scatter_dimension=0, tiled=True)  113 us
    psum x2, blocking collectives, shards(): lax.psum((jnp.sum(valid_mask * mismatch * mismatch), jnp.sum(valid_mask))...  81.3 us
    psum x1, blocking collectives, shards(): lax.psum((query_weight_grad, query_bias_grad, key_weight_grad, value_weig...  60.7 us
    dynamic_update_slice x24, local copies, waits for them, and re-layouts, shards(): lax.scan(whole_block, zero_rows, offsets)  55.3 us
  transfers between devices with their start and end apart: 17, of which 13 were waited for; matrix products, arithmetic and copies ran while one was open for 12% of the time, Pallas kernels for 0%

commit v1 on v0

v1 whole, which is shorter than its diff:
```python
from functools import partial
import math

import jax
import jax.numpy as jnp
from jax import lax
from jax.experimental import pallas as pl
from jax.experimental.pallas import tpu as pltpu
from jax.sharding import PartitionSpec as P

H = 12
head_size = 64
head_splits = 4
norm_eps = 1e-12
log_two = math.log(2.0)
masked_score = -1e30
low_type = jnp.bfloat16
wide_type = jnp.float32
score_scale = 1.0 / (log_two * math.sqrt(head_size))
vmem_bytes = 56 * 1024 * 1024

plain_dims = (((1,), (0,)), ((), ()))
back_dims = (((1,), (1,)), ((), ()))
weight_dims = (((0,), (0,)), ((), ()))


def product(left_op, right_op, dims=plain_dims):
    return lax.dot_general(left_op, right_op, dims, preferred_element_type=wide_type)


def layer_norm(hidden, norm_gain, norm_shift):
    centre = hidden - jnp.mean(hidden, axis=-1, keepdims=True)
    inverse = lax.rsqrt(jnp.mean(centre * centre, axis=-1, keepdims=True) + norm_eps)
    return centre * inverse * norm_gain + norm_shift


def gelu_exact(hidden_pre):
    return jax.nn.gelu(hidden_pre, approximate=False)


def lanes_of(shape):
    return lax.broadcasted_iota(jnp.int32, shape, 1)


def attend_kernel(head_count, key_rows, q_ref, kv_ref, aug_ref, low_ref, wide_ref, stat_ref):
    rows = q_ref.shape[0]
    length = kv_ref.shape[0]
    lane = lanes_of((rows, 128))
    q_aug = jnp.where(lane == 0, 1.0, 0.0).astype(low_type)
    stats = jnp.zeros((rows, 128), wide_type)
    outs = []
    for head in range(head_count):
        cols = pl.ds(head * 128, 128)
        q_ext = jnp.concatenate([q_ref[:, cols], q_aug], axis=1)
        top = None
        for start in range(0, length, key_rows):
            part = pl.ds(start, key_rows)
            kv_ext = jnp.concatenate([kv_ref[part, cols], aug_ref[part, :]], axis=1)
            scores = product(q_ext, kv_ext, back_dims)
            new_top = jnp.floor(jnp.max(scores, axis=1, keepdims=True))
            if top is not None:
                new_top = jnp.maximum(top, new_top)
            weights = jnp.exp2(scores - new_top).astype(low_type)
            part_sum = product(weights, kv_ext)
            if top is None:
                accum = part_sum
            else:
                accum = accum * jnp.exp2(top - new_top) + part_sum
            top = new_top
        total = accum[:, 129:130]
        outs.append(accum[:, :128] / total)
        stats = jnp.where(lane == head, top, stats)
        stats = jnp.where(lane == head_count + head, total, stats)
    tiles = []
    for head in range(0, head_count, 2):
        first = pltpu.roll(outs[head], 64, 1)
        if head + 1 < head_count:
            tiles.append(jnp.where(lane < 64, first, outs[head + 1]))
        else:
            tiles.append(first[:, :64])
    context = jnp.concatenate(tiles, axis=1)
    wide_ref[...] = context
    low_ref[...] = context.astype(low_type)
    stat_ref[...] = stats


def attend(q_pad, kv_all, aug, head_count):
    query_rows = q_pad.shape[0]
    length = kv_all.shape[0]
    tile = 256
    width = head_count * head_size
    whole = lambda i: (0, 0)
    by_tile = lambda i: (i, 0)
    work = query_rows * length * head_count
    return pl.pallas_call(
        partial(attend_kernel, head_count, math.gcd(length, 2048)),
        grid=(query_rows // tile,),
        in_specs=[
            pl.BlockSpec((tile, q_pad.shape[1]), by_tile),
            pl.BlockSpec(kv_all.shape, whole),
            pl.BlockSpec(aug.shape, whole),
        ],
        out_specs=[
            pl.BlockSpec((tile, width), by_tile),
            pl.BlockSpec((tile, width), by_tile),
            pl.BlockSpec((tile, 128), by_tile),
        ],
        out_shape=[
            jax.ShapeDtypeStruct((query_rows, width), low_type),
            jax.ShapeDtypeStruct((query_rows, width), wide_type),
            jax.ShapeDtypeStruct((query_rows, 128), wide_type),
        ],
        cost_estimate=pl.CostEstimate(
            flops=work * 1024, bytes_accessed=8 * 1024 * 1024, transcendentals=work
        ),
        compiler_params=pltpu.CompilerParams(vmem_limit_bytes=vmem_bytes),
    )(q_pad, kv_all, aug)


def split_three(number):
    first = number.astype(low_type).astype(wide_type)
    second = (number - first).astype(low_type).astype(wide_type)
    return first, second, number - first - second


def attend_back_kernel(
    head, head_count, query_part,
    q_ref, stat_ref, grad_ref, context_ref, kv_ref, aug_ref, keys_ref,
    kv_grad_ref, q_grad_ref, q_ext, g_ext,
):
    rows = kv_ref.shape[0]
    query_rows = q_ref.shape[0]

    @pl.when(pl.program_id(0) == 0)
    def _():
        q_grad_ref[...] = jnp.zeros_like(q_grad_ref)
        for start in range(0, query_rows, 256):
            part = pl.ds(start, 256)
            lane = lanes_of((256, 128))
            stats = stat_ref[part, :]
            top = stats[:, head : head + 1]
            total = stats[:, head_count + head : head_count + head + 1]
            begin = head // 2 * 128
            if head % 2 == 0 and head == head_count - 1:
                spare = jnp.zeros((256, 64), wide_type)
                grad = jnp.concatenate([spare, grad_ref[part, begin:].astype(wide_type)], axis=1)
                context = jnp.concatenate([spare, context_ref[part, begin:]], axis=1)
            else:
                grad = grad_ref[part, begin : begin + 128].astype(wide_type)
                context = context_ref[part, begin : begin + 128]
                if head % 2 == 0:
                    grad = pltpu.roll(grad, 64, 1)
                    context = pltpu.roll(context, 64, 1)
            grad = jnp.where(lane >= 64, grad, 0.0)
            delta = jnp.sum(grad * context, axis=1, keepdims=True) / total
            q_more = jnp.where(lane == 0, 1.0, 0.0)
            g_more = jnp.zeros((256, 128), wide_type)
            for place, (of_top, of_delta) in enumerate(zip(split_three(top), split_three(delta))):
                q_more = jnp.where(lane == place + 1, -of_top, q_more)
                g_more = jnp.where(lane == place + 1, -of_delta, g_more)
            q_ext[part, :128] = q_ref[part, :]
            q_ext[part, 128:] = q_more.astype(low_type)
            g_ext[part, :128] = (grad / total).astype(low_type)
            g_ext[part, 128:] = g_more.astype(low_type)

    kv_ext = jnp.concatenate([kv_ref[...], aug_ref[...]], axis=1)
    accum = jnp.zeros((rows, 128), wide_type)
    for start in range(0, query_rows, query_part):
        part = pl.ds(start, query_part)
        q_part = q_ext[part, :]
        g_part = g_ext[part, :]
        weights = jnp.exp2(product(kv_ext, q_part, back_dims))
        along_values = product(kv_ext, g_part, back_dims)
        grad_scores = (weights * along_values).astype(low_type)
        accum = accum + product(weights.astype(low_type), g_part[:, :128])
        accum = accum + product(grad_scores, q_part[:, :128])
        q_grad_ref[:, part] += product(keys_ref[...], grad_scores)
    lane = lanes_of((rows, 128))
    kv_grad_ref[...] = (accum * jnp.where(lane < 64, log_two, 1.0)).astype(low_type)


def attend_back(head, head_count, q_pad, stats, grad_context, context, kv_all, aug, kv_turned):
    query_rows = q_pad.shape[0]
    length = kv_all.shape[0]
    rows = math.gcd(length, 1024)
    width = grad_context.shape[1]
    whole = lambda i: (0, 0)
    work = query_rows * length
    return pl.pallas_call(
        partial(attend_back_kernel, head, head_count, 512),
        grid=(length // rows,),
        in_specs=[
            pl.BlockSpec((query_rows, 128), lambda i: (0, head)),
            pl.BlockSpec((query_rows, 128), whole),
            pl.BlockSpec((query_rows, width), whole),
            pl.BlockSpec((query_rows, width), whole),
            pl.BlockSpec((rows, 128), lambda i: (i, head)),
            pl.BlockSpec((rows, 128), lambda i: (i, 0)),
            pl.BlockSpec((64, rows), lambda i: (2 * head, i)),
        ],
        out_specs=[
            pl.BlockSpec((rows, 128), lambda i: (i, 0)),
            pl.BlockSpec((64, query_rows), whole),
        ],
        out_shape=[
            jax.ShapeDtypeStruct((length, 128), low_type),
            jax.ShapeDtypeStruct((64, query_rows), wide_type),
        ],
        scratch_shapes=[
            pltpu.VMEM((query_rows, 256), low_type),
            pltpu.VMEM((query_rows, 256), low_type),
        ],
        cost_estimate=pl.CostEstimate(
            flops=work * 2560, bytes_accessed=8 * 1024 * 1024, transcendentals=work
        ),
        compiler_params=pltpu.CompilerParams(vmem_limit_bytes=vmem_bytes),
    )(q_pad, stats, grad_context, context, kv_all, aug, kv_turned)


class Layout:
    def __init__(self):
        self.ctx = lax.axis_size("ctx")
        self.fsdp = lax.axis_size("fsdp")
        self.ring = self.ctx // head_splits
        self.group = lax.axis_index("ctx") // self.ring
        self.place = lax.axis_index("ctx") % self.ring
        self.row = lax.axis_index("fsdp")
        self.bits = [1 << k for k in reversed(range(self.ring.bit_length() - 1))]

    def shift(self, block, by):
        pairs = [(i, (i + by * self.ring) % self.ctx) for i in range(self.ctx)]
        return lax.ppermute(block, "ctx", pairs)

    def swap(self, block, bit):
        return lax.ppermute(block, "ctx", [(i, i ^ bit) for i in range(self.ctx)])

    def bit_of(self, bit):
        return (self.place // bit) % 2

    def across(self, block):
        return lax.ppermute(block, "fsdp", [(0, 1), (1, 0)])

    def gather_rows(self, shard):
        rows = shard.shape[0]
        if self.fsdp != 2:
            return lax.all_gather(shard, "fsdp", axis=0, tiled=True)
        half = rows // 2
        core = self.bit_of(1)
        mine = self.across(lax.dynamic_slice_in_dim(shard, core * half, half, 0))
        other = self.swap(mine, 1)
        whole = jnp.zeros((rows * 2,) + shard.shape[1:], shard.dtype)
        far = (1 - self.row) * rows
        whole = lax.dynamic_update_slice_in_dim(whole, shard, self.row * rows, 0)
        whole = lax.dynamic_update_slice_in_dim(whole, mine, far + core * half, 0)
        return lax.dynamic_update_slice_in_dim(whole, other, far + (1 - core) * half, 0)

    def gather_small(self, shard):
        if self.fsdp != 2:
            return lax.all_gather(shard, "fsdp", axis=0, tiled=False)
        other = self.across(shard)
        return jnp.where(
            self.row == 0, jnp.stack([shard, other]), jnp.stack([other, shard])
        )

    def to_far(self, blocks):
        twice = jnp.concatenate([blocks, blocks], axis=0)
        return lax.dynamic_slice_in_dim(twice, self.group, head_splits, 0)

    def to_near(self, blocks):
        twice = jnp.concatenate([blocks, blocks], axis=0)
        return lax.dynamic_slice_in_dim(twice, head_splits - self.group, head_splits, 0)

    def reduce_bit(self, array, bit, axis=0):
        half = array.shape[axis] // 2
        mine = self.bit_of(bit)
        keep = lax.dynamic_slice_in_dim(array, mine * half, half, axis)
        give = lax.dynamic_slice_in_dim(array, (1 - mine) * half, half, axis)
        got = self.swap(give.astype(low_type), bit)
        return keep.astype(wide_type) + got.astype(wide_type)

    def gather_bit(self, array, bit):
        other = self.swap(array, bit)
        return jnp.where(
            self.bit_of(bit) == 0,
            jnp.concatenate([array, other]),
            jnp.concatenate([other, array]),
        )

    def reduce_rows(self, array):
        if self.fsdp != 2:
            summed = lax.psum_scatter(
                array.astype(wide_type), "fsdp", scatter_dimension=0, tiled=True
            )
            return summed[0]
        keep = lax.dynamic_index_in_dim(array, self.row, 0, keepdims=False)
        give = lax.dynamic_index_in_dim(array, 1 - self.row, 0, keepdims=False)
        got = self.across(give.astype(low_type))
        return keep.astype(wide_type) + got.astype(wide_type)


def shards(
    layer_input,
    teacher_states,
    seq_lengths,
    query_weight,
    query_bias,
    key_weight,
    value_weight,
    value_bias,
    out_weight,
    out_bias,
    attn_gain,
    attn_shift,
    inner_weight,
    inner_bias,
    outer_weight,
    outer_bias,
    final_gain,
    final_shift,
):
    at = Layout()
    seg_rows, groups, width = layer_input.shape
    shard_rows = query_weight.shape[0]
    ff_rows = outer_weight.shape[0]
    ff_width = inner_weight.shape[1]
    heads = H // head_splits
    cols = heads * head_size
    tokens = layer_input.reshape(seg_rows, width)

    blocks = [tokens] + [at.shift(tokens, s) for s in range(1, head_splits)]

    def group_cols(weight):
        return lax.dynamic_slice_in_dim(weight, at.group * cols, cols, 1)

    w_qkv = at.gather_small(
        jnp.concatenate(
            [group_cols(query_weight), group_cols(key_weight), group_cols(value_weight)], axis=1
        ).reshape(-1)
    ).reshape(width, 3, heads, head_size)
    vectors = at.gather_small(
        jnp.concatenate(
            [
                query_bias, value_bias, out_bias, attn_gain, attn_shift,
                outer_bias, final_gain, final_shift, inner_bias,
            ]
        )
    ).astype(wide_type)
    vector = lambda k: vectors[:, k * shard_rows : (k + 1) * shard_rows].reshape(-1)
    b_query, b_value, b_out, g_attn, s_attn, b_outer, g_final, s_final = map(vector, range(8))
    b_inner = vectors[:, 8 * shard_rows :].reshape(-1)
    w_out = at.gather_rows(out_weight)
    w_inner = at.gather_rows(inner_weight)
    w_outer = at.gather_rows(outer_weight)
    own_count = jnp.sum(seq_lengths).astype(wide_type)
    if at.fsdp == 2:
        valid_count = own_count + at.across(own_count.reshape(1))[0]
    else:
        valid_count = lax.psum(own_count, "fsdp")

    w_query, w_key, w_value = (w_qkv[:, k] for k in range(3))
    w_pack = jnp.concatenate(
        [
            jnp.pad(w_query, ((0, 0), (0, 0), (0, head_size))).reshape(width, 2 * cols),
            jnp.concatenate([w_key, w_value], axis=2).reshape(width, 2 * cols),
        ],
        axis=1,
    )
    group_bias = lambda b: lax.dynamic_slice_in_dim(b, at.group * cols, cols, 0).reshape(
        heads, head_size
    )
    q_bias = jnp.pad(group_bias(b_query), ((0, 0), (0, head_size))).reshape(-1)
    kv_bias = jnp.pad(group_bias(b_value), ((0, 0), (head_size, 0))).reshape(-1)
    x_line = jnp.concatenate(blocks, axis=0)
    projected = product(x_line, w_pack)
    q_pad = ((projected[:, : 2 * cols] + q_bias) * score_scale).astype(low_type)
    kv_all = (projected[:, 2 * cols :] + kv_bias).astype(low_type)
    codes = [0]
    for bit in at.bits:
        kv_all = jnp.concatenate([kv_all, at.swap(kv_all, bit)], axis=0)
        codes = codes + [code ^ bit for code in codes]
    length = kv_all.shape[0]
    source = jnp.concatenate(
        [
            ((at.group - jnp.arange(head_splits)) % head_splits) * at.ring + (at.place ^ code)
            for code in codes
        ]
    )
    position = (source[:, None] * seg_rows + jnp.arange(seg_rows)[None, :]).reshape(-1, 1)
    lane = lax.broadcasted_iota(jnp.int32, (length, 128), 1)
    mask = jnp.where(position < seq_lengths[0], 0.0, masked_score)
    aug = jnp.where(lane == 0, mask, jnp.where(lane < 4, 1.0, 0.0)).astype(low_type)

    context_low, context_wide, stats = attend(q_pad, kv_all, aug, heads)
    kv_turned = kv_all.T

    line = context_low.reshape(head_splits, seg_rows, cols)
    back = [line[0]] + [at.shift(line[s], -s) for s in range(1, head_splits)]
    context_low = (
        at.to_near(jnp.stack(back)).transpose(1, 0, 2).reshape(seg_rows, width)
    )
    attn_out = product(context_low, w_out) + b_out
    pre_norm = tokens.astype(wide_type) + attn_out
    normed, attn_pull = jax.vjp(layer_norm, pre_norm, g_attn, s_attn)
    normed_low = normed.astype(low_type)
    hidden_pre = product(normed_low, w_inner) + b_inner
    act, gelu_pull = jax.vjp(gelu_exact, hidden_pre)
    act_low = act.astype(low_type)
    branch = product(act_low, w_outer) + b_outer
    output, final_pull = jax.vjp(layer_norm, normed + branch, g_final, s_final)
    target = teacher_states.reshape(seg_rows, width).astype(wide_type)
    own_position = lax.axis_index("ctx") * seg_rows + jnp.arange(seg_rows)[:, None]
    valid_mask = (own_position < seq_lengths[0]).astype(wide_type)
    mismatch = output - target
    total_sq = jnp.sum(valid_mask * mismatch * mismatch)
    token_total = seg_rows * groups * at.ctx * at.fsdp
    grad_out = 2.0 * valid_mask * mismatch * (token_total / valid_count)
    grad_mid, final_gain_grad, final_shift_grad = final_pull(grad_out)
    grad_branch = grad_mid.astype(low_type)
    outer_bias_grad = jnp.sum(grad_branch, axis=0, dtype=wide_type)
    outer_weight_grad = product(act_low, grad_branch, weight_dims)
    grad_hidden = gelu_pull(product(grad_branch, w_outer, back_dims))[0].astype(low_type)
    inner_bias_grad = jnp.sum(grad_hidden, axis=0, dtype=wide_type)
    inner_weight_grad = product(normed_low, grad_hidden, weight_dims)
    grad_normed = grad_mid + product(grad_hidden, w_inner, back_dims)
    grad_sum, attn_gain_grad, attn_shift_grad = attn_pull(grad_normed)
    grad_attn = grad_sum.astype(low_type)
    out_bias_grad = jnp.sum(grad_attn, axis=0, dtype=wide_type)
    out_weight_grad = product(context_low, grad_attn, weight_dims)
    grad_context = product(grad_attn, w_out, back_dims).astype(low_type)

    line = at.to_far(grad_context.reshape(seg_rows, head_splits, cols).transpose(1, 0, 2))
    grad_line = jnp.concatenate(
        [line[0]] + [at.shift(line[s], s) for s in range(1, head_splits)], axis=0
    )
    kv_grads, q_grads = [], []
    for head in range(heads):
        kv_grad, q_grad = attend_back(
            head, heads, q_pad, stats, grad_line, context_wide, kv_all, aug, kv_turned
        )
        for bit in reversed(at.bits):
            half = kv_grad.shape[0] // 2
            got = at.swap(kv_grad[half:], bit)
            kv_grad = (kv_grad[:half].astype(wide_type) + got.astype(wide_type)).astype(low_type)
        kv_grads.append(kv_grad)
        q_grads.append(q_grad)
    q_rows = (jnp.concatenate(q_grads, axis=0).T * 0.125).astype(low_type)
    kv_rows = jnp.stack(kv_grads, axis=1).reshape(-1, heads, 2, head_size)
    rows = jnp.concatenate(
        [q_rows, kv_rows[:, :, 0].reshape(-1, cols), kv_rows[:, :, 1].reshape(-1, cols)], axis=1
    )

    qkv_grad = product(x_line, rows, weight_dims)
    bias_rows = jnp.sum(rows, axis=0, dtype=wide_type)
    line = rows.reshape(head_splits, seg_rows, 3 * cols)
    near = at.to_near(
        jnp.stack([line[0]] + [at.shift(line[s], -s) for s in range(1, head_splits)])
    ).reshape(head_splits, seg_rows, 3, cols)
    all_rows = near.transpose(1, 2, 0, 3).reshape(seg_rows, 3 * width)
    w_all = jnp.concatenate([at.gather_rows(w) for w in (query_weight, key_weight, value_weight)], axis=1)
    input_grad = grad_sum + product(all_rows, w_all, back_dims)

    def spread(weight_rows):
        low = weight_rows.astype(low_type)
        if at.ring > 1:
            low = at.reduce_bit(low, 1, axis=1).astype(low_type)
        kept = at.reduce_rows(low).astype(low_type)
        same_core = [[i for i in range(at.ctx) if i % 2 == c] for c in range(2)]
        part = lax.psum_scatter(
            kept, "ctx", scatter_dimension=0, tiled=True, axis_index_groups=same_core
        )
        full = lax.all_gather(part, "ctx", axis=0, tiled=True, axis_index_groups=same_core)
        return at.gather_bit(full, 1).astype(wide_type)

    outer_weight_grad = spread(outer_weight_grad.reshape(at.fsdp, ff_rows, width))
    inner_weight_grad = spread(inner_weight_grad.reshape(at.fsdp, shard_rows, ff_width))
    out_weight_grad = spread(out_weight_grad.reshape(at.fsdp, shard_rows, width))

    part = qkv_grad.reshape(at.fsdp, shard_rows, 3 * cols)
    for bit in reversed(at.bits):
        part = at.reduce_bit(part, bit, axis=1)
    part = at.reduce_rows(part).astype(low_type)
    from_groups = at.to_near(
        jnp.stack([part] + [at.shift(part, -s) for s in range(1, head_splits)])
    ).transpose(1, 0, 2)
    whole = from_groups
    for bit in at.bits:
        whole = at.gather_bit(whole, bit)
    whole = whole.reshape(shard_rows, head_splits, 3, cols).transpose(0, 2, 1, 3)
    whole = whole.reshape(shard_rows, 3, width).astype(wide_type)

    placed_bias = lax.dynamic_update_slice(
        jnp.zeros((3, width), wide_type), bias_rows.reshape(3, cols), (0, at.group * cols)
    )
    small = jnp.concatenate(
        [
            placed_bias[0], placed_bias[2], out_bias_grad, attn_gain_grad, attn_shift_grad,
            outer_bias_grad, final_gain_grad, final_shift_grad, inner_bias_grad,
            jnp.full((128,), total_sq),
        ]
    )
    small = lax.psum(small, ("ctx", "fsdp"))
    small_part = lambda k: lax.dynamic_slice_in_dim(
        small, k * width + at.row * shard_rows, shard_rows, 0
    )
    (
        query_bias_grad, value_bias_grad, out_bias_grad, attn_gain_grad, attn_shift_grad,
        outer_bias_grad, final_gain_grad, final_shift_grad,
    ) = map(small_part, range(8))
    inner_bias_grad = lax.dynamic_slice_in_dim(small, 8 * width + at.row * ff_rows, ff_rows, 0)
    distill_loss = small[8 * width + ff_width] / (width * valid_count)
    return (
        distill_loss,
        output.reshape(seg_rows, groups, width),
        input_grad.reshape(seg_rows, groups, width),
        whole[:, 0],
        query_bias_grad,
        whole[:, 1],
        whole[:, 2],
        value_bias_grad,
        out_weight_grad,
        out_bias_grad,
        attn_gain_grad,
        attn_shift_grad,
        inner_weight_grad,
        inner_bias_grad,
        outer_weight_grad,
        outer_bias_grad,
        final_gain_grad,
        final_shift_grad,
    )


def solution(mesh):
    states = P("ctx", "fsdp", None)
    matrix = P("fsdp", None)
    vector = P("fsdp")
    placed = (
        states, states, vector,
        matrix, vector, matrix, matrix, vector, matrix, vector, vector, vector,
        matrix, vector, matrix, vector, vector, vector,
    )
    return jax.shard_map(
        shards,
        mesh=mesh,
        in_specs=placed,
        out_specs=(P(), states, states) + placed[3:],
        check_vma=False,
    )
```

time: 1590 us -> 657 us (0.41)
  waiting for transfers between devices: 868 us -> 215 us
  matrix products: 217 us -> 37.4 us
  blocking collectives: 192 us -> 70.4 us
  Pallas kernels: 0 us -> 68 us
  starting transfers between devices: 0.93 us -> 54.9 us
  local copies, waits for them, and re-layouts: 167 us -> 127 us
  loops' own time: 32.7 us -> 0 us
  other arithmetic: 84.6 us -> 55.7 us
    reduce_scatter x8 -> x3, waiting for transfers between devices: 618 us -> 44.4 us  [spread(): lax.psum_scatter(kept, 'ctx', scatter_dimension=0, tiled=True, axis_index...]
    dot_general x74 -> x11, matrix products: 217 us -> 34.7 us  [product(): lax.dot_general(left_op, right_op, dims, preferred_element_type=wide_type)]
    psum x1 -> x0, waiting for transfers between devices: 143 us -> none  [shards(): lax.psum((query_weight_grad, query_bias_grad, key_weight_grad, value_weig...]
    ppermute x0 -> x52, waiting for transfers between devices: none -> 122 us  [the longest x13 66.8 us: across(): return lax.ppermute(block, 'fsdp', [(0, 1), (1, 0)])]
    psum x3 -> x1, blocking collectives: 142 us -> 39 us  [shards(): small = lax.psum(small, ('ctx', 'fsdp'))]
    pallas_call x0 -> x4, Pallas kernels: none -> 68 us  [the longest x3 47 us: attend_back(): pl.pallas_call(partial(attend_back_kernel, head, head_count, 512), grid=(...]
    ppermute x0 -> x52, starting transfers between devices: none -> 54.7 us  [the longest x13 24.6 us: across(): return lax.ppermute(block, 'fsdp', [(0, 1), (1, 0)])]
    all_gather x8 -> x2, waiting for transfers between devices: 102 us -> 47.8 us  [spread(): lax.all_gather(part, 'ctx', axis=0, tiled=True, axis_index_groups=same_core)]
  transfers between devices with their start and end apart: 17 -> 57, of which waited for: 13 -> 18; matrix products, arithmetic and copies ran while one was open for 12% -> 26% of each run, Pallas kernels for 0% -> 7%
where the time goes in v1:
time: 657 us; the launch traced here: 646 us
  waiting for transfers between devices  215 us (33%)
  local copies, waits for them, and re-layouts  127 us (19%)
  blocking collectives  70.4 us (11%)
  Pallas kernels  68 us (10%)
  other arithmetic  55.7 us (8%)
  starting transfers between devices  54.9 us (8%)
  matrix products  37.4 us (6%)
  between operations  18.2 us (3%)
    ppermute x13, waiting for transfers between devices, across(): return lax.ppermute(block, 'fsdp', [(0, 1), (1, 0)])  66.8 us
    all_gather x2, waiting for transfers between devices, spread(): lax.all_gather(part, 'ctx', axis=0, tiled=True, axis_index_groups=same_core)  47.8 us
    unnamed x157, local copies, waits for them, and re-layouts  47.3 us
    pallas_call x3, Pallas kernels, attend_back(): pl.pallas_call(partial(attend_back_kernel, head, head_count, 512), grid=(...  47 us
    reduce_scatter x3, waiting for transfers between devices, spread(): lax.psum_scatter(kept, 'ctx', scatter_dimension=0, tiled=True, axis_index...  44.4 us
    ppermute x15, waiting for transfers between devices, shift(): return lax.ppermute(block, 'ctx', pairs)  39.3 us
    psum x1, blocking collectives, shards(): small = lax.psum(small, ('ctx', 'fsdp'))  39 us
    dot_general x11, matrix products, product(): lax.dot_general(left_op, right_op, dims, preferred_element_type=wide_type)  34.7 us
  transfers between devices with their start and end apart: 57, of which 18 were waited for; matrix products, arithmetic and copies ran while one was open for 26% of the time, Pallas kernels for 7%

profile of v1, /device:TPU:0, one launch (start us, length us, event | category | flops | bytes accessed | tf_op | source)
XLA Modules:
  0.0 646.1 jit_solution(10298847187751314068)
XLA Ops:
  7.4 5.1 collective-permute-start.2
  63.9 4.6 broadcast_select_fusion
  75.5 13.6 %collective-permute-start.16 = (f32[1]{0:T(128)}, f32[1]{0:T(128)}, u32[]{:S(2)}, u32[]{:S(2)}) collective-permute-start(f32[1]{0:T(128)} %bitcast.16), channel_id=1, source_target_pairs={{0,1},{1,0},{2,3},{3,2},{4,5},{5,4},{6,7},{7,6},{8,9},{9,8},{10,11... | collective-permute-start | bytes 20 | tf_op jit(solution)/shard_map/ppermute | solution.py:241
  104.0 20.5 %collective-permute-done.33 = bf16[192,768]{1,0:T(8,128)(2,1)S(1)} collective-permute-done((bf16[192,768]{1,0:T(8,128)(2,1)}, bf16[192,768]{1,0:T(8,128)(2,1)S(1)}, u32[]{:S(2)}, u32[]{:S(2)}) %collective-permute-start.33) | collective-permute-done | bytes 294944 | tf_op jit(solution)/shard_map/ppermute | solution.py:241
  125.8 4.9 collective-permute-done.31
  152.3 21.0 %shard_map.313 = (bf16[1024,192]{1,0:T(8,128)(2,1)}, f32[1024,192]{1,0:T(8,128)}, f32[1024,128]{1,0:T(8,128)}) custom-call(bf16[1024,384]{1,0:T(8,128)(2,1)} %get-tuple-element.121.q_ref, bf16[4096,384]{1,0:T(8,128)(2,1)} %copy.84.kv_ref, bf16[4096,128]{1,0:T(8,128)(2,1)} %select_convert_fusion.aug_ref), custom_call_target="tpu_custom_call" | custom-call | flops 12884901888 | bytes 8388608 | tf_op jit(solution)/shard_map/pallas_call | solution.py:95
  174.6 3.0 collective-permute-start.7
  181.5 9.0 %collective-permute-done.8 = bf16[256,192]{1,0:T(8,128)(2,1)S(1)} collective-permute-done((bf16[256,192]{1,0:T(8,128)(2,1)S(1)}, bf16[256,192]{1,0:T(8,128)(2,1)S(1)}, u32[]{:S(2)}, u32[]{:S(2)}) %collective-permute-start.8) | collective-permute-done | bytes 98336 | tf_op jit(solution)/shard_map/ppermute | solution.py:232
  192.7 10.3 %multiply_convert_fusion = (bf16[256,3072]{1,0:T(8,128)(2,1)S(1)}, f32[256,3072]{1,0:T(8,128)S(1)}, f32[256,3072]{1,0:T(8,128)S(1)}) fusion(f32[3072]{0:T(1024)S(1)} %add.476, bf16[768,3072]{1,0:T(8,128)(2,1)} %constant_dynamic-update-slice_fusion.13, f32[256,768]{1,0:T(8,128)S(1)} %get-tuple-element.155, f32[768]{0:T(1024)S(1)} %add.473, ...), kind=kOutput, calls=%fused_computation.17 | convolution fusion | flops 1260847104 | bytes 13389824 | tf_op jit(solution)/shard_map/dot_general | solution.py:28
  210.2 4.6 multiply_reduce_fusion.1
  214.8 3.8 convolution_convert_fusion.1
  218.6 3.6 convolution_convert_fusion
  236.2 3.3 collective-permute-done.18
  240.4 15.8 %shard_map.316 = (bf16[4096,128]{1,0:T(8,128)(2,1)}, f32[64,1024]{1,0:T(8,128)}) custom-call(bf16[1024,384]{1,0:T(8,128)(2,1)} %get-tuple-element.121.q_ref, f32[1024,128]{1,0:T(8,128)} %get-tuple-element.27.stat_ref, bf16[1024,192]{1,0:T(8,128)(2,1)} %pad_maximum_fusion.6.grad_ref, f32[1024,192]{1,0:T(8,128)} %get-tuple-element.29.context_ref, ...), custom_call_target="tpu_custom_call" | custom-call | flops 10737418240 | bytes 8388608 | tf_op jit(solution)/shard_map/pallas_call | solution.py:189
  258.1 15.2 %shard_map.315 = (bf16[4096,128]{1,0:T(8,128)(2,1)}, f32[64,1024]{1,0:T(8,128)}) custom-call(bf16[1024,384]{1,0:T(8,128)(2,1)} %get-tuple-element.121.q_ref, f32[1024,128]{1,0:T(8,128)} %get-tuple-element.27.stat_ref, bf16[1024,192]{1,0:T(8,128)(2,1)} %pad_maximum_fusion.6.grad_ref, f32[1024,192]{1,0:T(8,128)} %get-tuple-element.29.context_ref, ...), custom_call_target="tpu_custom_call" | custom-call | flops 10737418240 | bytes 8388608 | tf_op jit(solution)/shard_map/pallas_call | solution.py:189
  275.9 16.0 %shard_map.314 = (bf16[4096,128]{1,0:T(8,128)(2,1)}, f32[64,1024]{1,0:T(8,128)}) custom-call(bf16[1024,384]{1,0:T(8,128)(2,1)} %get-tuple-element.121.q_ref, f32[1024,128]{1,0:T(8,128)} %get-tuple-element.27.stat_ref, bf16[1024,192]{1,0:T(8,128)(2,1)} %pad_maximum_fusion.6.grad_ref, f32[1024,192]{1,0:T(8,128)} %get-tuple-element.29.context_ref, ...), custom_call_target="tpu_custom_call" | custom-call | flops 10737418240 | bytes 8388608 | tf_op jit(solution)/shard_map/pallas_call | solution.py:189
  305.6 20.0 %collective-permute-done.47 = bf16[192,3072]{1,0:T(8,128)(2,1)S(1)} collective-permute-done((bf16[192,3072]{1,0:T(8,128)(2,1)S(1)}, bf16[192,3072]{1,0:T(8,128)(2,1)S(1)}, u32[]{:S(2)}, u32[]{:S(2)}) %collective-permute-start.47) | collective-permute-done | bytes 1179680 | tf_op jit(solution)/shard_map/ppermute | solution.py:241
  332.8 3.0 add_convert_fusion
  348.1 15.6 %collective-permute-done.50 = bf16[768,768]{1,0:T(8,128)(2,1)} collective-permute-done((bf16[768,768]{1,0:T(8,128)(2,1)}, bf16[768,768]{1,0:T(8,128)(2,1)}, u32[]{:S(2)}, u32[]{:S(2)}) %collective-permute-start.50) | collective-permute-done | bytes 1179680 | tf_op jit(solution)/shard_map/ppermute | solution.py:241
  378.0 39.0 %psum.7 = f32[9344]{0:T(1024)S(1)} all-reduce(f32[9344]{0:T(1024)} %constant_dynamic-update-slice_fusion.21), channel_id=1, replica_groups=mesh['ctx'=16,'fsdp'=2] {'ctx','fsdp'}, use_global_device_ids=true, to_apply=%region_17.18 | all-reduce | flops 9344 | bytes 74752 | tf_op jit(solution)/shard_map/psum | solution.py:501
  432.1 16.3 %collective-permute-done.27 = bf16[256,576]{0,1:T(8,128)(2,1)S(1)} collective-permute-done((bf16[256,576]{0,1:T(8,128)(2,1)S(1)}, bf16[256,576]{0,1:T(8,128)(2,1)S(1)}, u32[]{:S(2)}, u32[]{:S(2)}) %collective-permute-start.27) | collective-permute-done | bytes 294944 | tf_op jit(solution)/shard_map/ppermute | solution.py:232
  452.2 5.6 collective-permute-done.36
  459.8 4.0 collective-permute-done.37
  469.5 6.1 collective-permute-done.39
  480.4 7.9 %collective-permute-done.41 = bf16[96,4,576]{2,0,1:T(8,128)(2,1)S(1)} collective-permute-done((bf16[96,4,576]{2,0,1:T(8,128)(2,1)S(1)}, bf16[96,4,576]{2,0,1:T(8,128)(2,1)S(1)}, u32[]{:S(2)}, u32[]{:S(2)}) %collective-permute-start.41) | collective-permute-done | bytes 442400 | tf_op jit(solution)/shard_map/ppermute | solution.py:235
  489.6 44.4 %reduce-scatter.4.cloned.1.call-done = bf16[24,768]{1,0:T(8,128)(2,1)} async-done(((bf16[192,768]{1,0:T(8,128)(2,1)}), bf16[24,768]{1,0:T(8,128)(2,1)}) %reduce-scatter.4.cloned.1.call-update) | async-done | bytes 36880 | tf_op jit(solution)/shard_map/reduce_scatter | solution.py:468
  534.0 31.3 %all_gather.9 = bf16[192,768]{1,0:T(8,128)(2,1)S(1)} all-gather(bf16[24,768]{1,0:T(8,128)(2,1)} %reduce-scatter.4.cloned.1.call-done), channel_id=1, replica_groups={{0,4,8,12,16,20,24,28},{2,6,10,14,18,22,26,30},{1,5,9,13,17,21,25,29},{..., dimensions={0}, use_global_device_ids=true | all-gather | bytes 331776 | tf_op jit(solution)/shard_map/all_gather | solution.py:471
  565.4 11.2 %all-gather.3.cloned.1.call-done = bf16[192,3072]{1,0:T(8,128)(2,1)} async-done(((bf16[24,3072]{1,0:T(8,128)(2,1)}), bf16[192,3072]{1,0:T(8,128)(2,1)}) %all-gather.3.cloned.1.call-update) | async-done | bytes 1179664 | tf_op jit(solution)/shard_map/all_gather | solution.py:471
  576.6 3.7 fusion.22
  582.1 36.6 %all-gather.5.cloned.1.call-done = bf16[768,768]{1,0:T(8,128)(2,1)} async-done(((bf16[96,768]{1,0:T(8,128)(2,1)}), bf16[768,768]{1,0:T(8,128)(2,1)}) %all-gather.5.cloned.1.call-update) | async-done | bytes 1179664 | tf_op jit(solution)/shard_map/all_gather | solution.py:471
  629.0 4.7 fusion.12
  633.7 4.6 fusion.13
  (432 shorter events, 219.2 us)
Async XLA Ops:
  7.3 444.1 %reduce-scatter.6.cloned.1.call-start = ((), (), s32[]{:S(2)}) async-start(), calls=%async_computation.4 | async-start | bytes 1327104 | tf_op jit(solution)/shard_map/reduce_scatter | solution.py:468
  7.4 68.2 %collective-permute-start.2 = (bf16[256,768]{1,0:T(8,128)(2,1)}, bf16[256,768]{1,0:T(8,128)(2,1)}, u32[]{:S(2)}, u32[]{:S(2)}) collective-permute-start(bf16[256,768]{1,0:T(8,128)(2,1)} %bitcast.202), channel_id=1, source_target_pairs={{0,24},{2,26},{4,28},{6,30},{8,0},{10,2},{12,4},{14,6},{16,8},{18,... | collective-permute-start | bytes 1179656 | tf_op jit(solution)/shard_map/ppermute | solution.py:232
  12.5 76.7 %collective-permute-start.1 = (bf16[256,768]{1,0:T(8,128)(2,1)}, bf16[256,768]{1,0:T(8,128)(2,1)}, u32[]{:S(2)}, u32[]{:S(2)}) collective-permute-start(bf16[256,768]{1,0:T(8,128)(2,1)} %bitcast.203), channel_id=1, source_target_pairs={{0,16},{2,18},{4,20},{6,22},{8,24},{10,26},{12,28},{14,30},{16,0},... | collective-permute-start | bytes 1179656 | tf_op jit(solution)/shard_map/ppermute | solution.py:232
  12.5 77.2 %collective-permute-start = (bf16[256,768]{1,0:T(8,128)(2,1)}, bf16[256,768]{1,0:T(8,128)(2,1)}, u32[]{:S(2)}, u32[]{:S(2)}) collective-permute-start(bf16[256,768]{1,0:T(8,128)(2,1)} %bitcast.204), channel_id=1, source_target_pairs={{0,8},{2,10},{4,12},{6,14},{8,16},{10,18},{12,20},{14,22},{16,24},... | collective-permute-start | bytes 1179656 | tf_op jit(solution)/shard_map/ppermute | solution.py:232
  18.2 43.7 %collective-permute-start.3 = (bf16[221184]{0:T(1024)(128)(2,1)}, bf16[221184]{0:T(1024)(128)(2,1)}, u32[]{:S(2)}, u32[]{:S(2)}) collective-permute-start(bf16[221184]{0:T(1024)(128)(2,1)} %reshape.275), channel_id=1, source_target_pairs={{0,1},{1,0},{2,3},{3,2},{4,5},{5,4},{6,7},{7,6},{8,9},{9,8},{10,11... | collective-permute-start | bytes 1327112 | tf_op jit(solution)/shard_map/ppermute | solution.py:241
  31.7 25.1 %collective-permute-start.4 = (bf16[4608]{0:T(1024)(128)(2,1)}, bf16[4608]{0:T(1024)(128)(2,1)}, u32[]{:S(2)}, u32[]{:S(2)}) collective-permute-start(bf16[4608]{0:T(1024)(128)(2,1)} %constant_dynamic-update-slice_fusion.19), channel_id=1, source_target_pairs={{0,1},{1,0},{2,3},{3,2},{4,5},{5,4},{6,7},{7,6},{8,9},{9,8},{10,11... | collective-permute-start | bytes 27656 | tf_op jit(solution)/shard_map/ppermute | solution.py:241
  56.7 45.0 %collective-permute-start.10 = (bf16[192,768]{1,0:T(8,128)(2,1)}, bf16[192,768]{1,0:T(8,128)(2,1)}, u32[]{:S(2)}, u32[]{:S(2)}) collective-permute-start(bf16[192,768]{1,0:T(8,128)(2,1)} %constant_dynamic-slice_fusion.9), channel_id=1, source_target_pairs={{0,1},{1,0},{2,3},{3,2},{4,5},{5,4},{6,7},{7,6},{8,9},{9,8},{10,11... | collective-permute-start | bytes 884744 | tf_op jit(solution)/shard_map/ppermute | solution.py:241
  61.9 72.0 %collective-permute-start.12 = (bf16[192,3072]{1,0:T(8,128)(2,1)}, bf16[192,3072]{1,0:T(8,128)(2,1)}, u32[]{:S(2)}, u32[]{:S(2)}) collective-permute-start(bf16[192,3072]{1,0:T(8,128)(2,1)} %constant_dynamic-slice_fusion.8), channel_id=1, source_target_pairs={{0,1},{1,0},{2,3},{3,2},{4,5},{5,4},{6,7},{7,6},{8,9},{9,8},{10,11... | collective-permute-start | bytes 3538952 | tf_op jit(solution)/shard_map/ppermute | solution.py:241
  75.5 24.7 %collective-permute-start.16 = (f32[1]{0:T(128)}, f32[1]{0:T(128)}, u32[]{:S(2)}, u32[]{:S(2)}) collective-permute-start(f32[1]{0:T(128)} %bitcast.16), channel_id=1, source_target_pairs={{0,1},{1,0},{2,3},{3,2},{4,5},{5,4},{6,7},{7,6},{8,9},{9,8},{10,11... | collective-permute-start | bytes 20 | tf_op jit(solution)/shard_map/ppermute | solution.py:241
  89.1 42.4 %collective-permute-start.14 = (bf16[768,768]{1,0:T(8,128)(2,1)}, bf16[768,768]{1,0:T(8,128)(2,1)}, u32[]{:S(2)}, u32[]{:S(2)}) collective-permute-start(bf16[768,768]{1,0:T(8,128)(2,1)} %constant_dynamic-slice_fusion.7), channel_id=1, source_target_pairs={{0,1},{1,0},{2,3},{3,2},{4,5},{5,4},{6,7},{7,6},{8,9},{9,8},{10,11... | collective-permute-start | bytes 3538952 | tf_op jit(solution)/shard_map/ppermute | solution.py:241
  96.8 35.2 %collective-permute-start.5 = (bf16[1024,384]{0,1:T(8,128)(2,1)S(1)}, bf16[1024,384]{0,1:T(8,128)(2,1)S(1)}, u32[]{:S(2)}, u32[]{:S(2)}) collective-permute-start(bf16[1024,384]{0,1:T(8,128)(2,1)S(1)} %add_convert_fusion.3), channel_id=1, source_target_pairs={{0,4},{2,6},{4,0},{6,2},{8,12},{10,14},{12,8},{14,10},{16,20},{18,... | collective-permute-start | bytes 2359304 | tf_op jit(solution)/shard_map/ppermute | solution.py:235
  100.3 24.3 %collective-permute-start.33 = (bf16[192,768]{1,0:T(8,128)(2,1)}, bf16[192,768]{1,0:T(8,128)(2,1)S(1)}, u32[]{:S(2)}, u32[]{:S(2)}) collective-permute-start(bf16[192,768]{1,0:T(8,128)(2,1)} %constant_dynamic-slice_fusion.3), channel_id=1, source_target_pairs={{0,1},{1,0},{2,3},{3,2},{4,5},{5,4},{6,7},{7,6},{8,9},{9,8},{10,11... | collective-permute-start | bytes 884744 | tf_op jit(solution)/shard_map/ppermute | solution.py:241
  101.8 29.0 %collective-permute-start.31 = (bf16[192,768]{1,0:T(8,128)(2,1)}, bf16[192,768]{1,0:T(8,128)(2,1)S(1)}, u32[]{:S(2)}, u32[]{:S(2)}) collective-permute-start(bf16[192,768]{1,0:T(8,128)(2,1)} %constant_dynamic-slice_fusion.4), channel_id=1, source_target_pairs={{0,1},{1,0},{2,3},{3,2},{4,5},{5,4},{6,7},{7,6},{8,9},{9,8},{10,11... | collective-permute-start | bytes 884744 | tf_op jit(solution)/shard_map/ppermute | solution.py:241
  232.4 64.3 %collective-permute-start.43 = (bf16[2,192,768]{2,1,0:T(8,128)(2,1)}, bf16[2,192,768]{2,1,0:T(8,128)(2,1)}, u32[]{:S(2)}, u32[]{:S(2)}) collective-permute-start(bf16[2,192,768]{2,1,0:T(8,128)(2,1)} %constant_dynamic-slice_fusion.2), channel_id=1, source_target_pairs={{0,2},{2,0},{4,6},{6,4},{8,10},{10,8},{12,14},{14,12},{16,18},{18,... | collective-permute-start | bytes 1769480 | tf_op jit(solution)/shard_map/ppermute | solution.py:235
  234.0 61.6 %collective-permute-start.46 = (bf16[2,192,3072]{2,1,0:T(8,128)(2,1)}, bf16[2,192,3072]{2,1,0:T(8,128)(2,1)S(1)}, u32[]{:S(2)}, u32[]{:S(2)}) collective-permute-start(bf16[2,192,3072]{2,1,0:T(8,128)(2,1)} %constant_dynamic-slice_fusion.1), channel_id=1, source_target_pairs={{0,2},{2,0},{4,6},{6,4},{8,10},{10,8},{12,14},{14,12},{16,18},{18,... | collective-permute-start | bytes 7077896 | tf_op jit(solution)/shard_map/ppermute | solution.py:235
  236.1 96.7 %collective-permute-start.49 = (bf16[2,768,768]{2,1,0:T(8,128)(2,1)}, bf16[2,768,768]{2,1,0:T(8,128)(2,1)}, u32[]{:S(2)}, u32[]{:S(2)}) collective-permute-start(bf16[2,768,768]{2,1,0:T(8,128)(2,1)} %constant_dynamic-slice_fusion), channel_id=1, source_target_pairs={{0,2},{2,0},{4,6},{6,4},{8,10},{10,8},{12,14},{14,12},{16,18},{18,... | collective-permute-start | bytes 7077896 | tf_op jit(solution)/shard_map/ppermute | solution.py:235
  258.1 42.2 %collective-permute-start.24 = (bf16[2048,128]{1,0:T(8,128)(2,1)}, bf16[2048,128]{1,0:T(8,128)(2,1)}, u32[]{:S(2)}, u32[]{:S(2)}) collective-permute-start(bf16[2048,128]{1,0:T(8,128)(2,1)} %slice.182), channel_id=1, source_target_pairs={{0,2},{2,0},{4,6},{6,4},{8,10},{10,8},{12,14},{14,12},{16,18},{18,... | collective-permute-start | bytes 1572872 | tf_op jit(solution)/shard_map/ppermute | solution.py:235
  275.4 26.7 %collective-permute-start.22 = (bf16[2048,128]{1,0:T(8,128)(2,1)}, bf16[2048,128]{1,0:T(8,128)(2,1)}, u32[]{:S(2)}, u32[]{:S(2)}) collective-permute-start(bf16[2048,128]{1,0:T(8,128)(2,1)} %slice.178), channel_id=1, source_target_pairs={{0,2},{2,0},{4,6},{6,4},{8,10},{10,8},{12,14},{14,12},{16,18},{18,... | collective-permute-start | bytes 1572872 | tf_op jit(solution)/shard_map/ppermute | solution.py:235
  295.7 32.9 %collective-permute-start.20 = (bf16[2048,128]{1,0:T(8,128)(2,1)}, bf16[2048,128]{1,0:T(8,128)(2,1)}, u32[]{:S(2)}, u32[]{:S(2)}) collective-permute-start(bf16[2048,128]{1,0:T(8,128)(2,1)} %slice.174), channel_id=1, source_target_pairs={{0,2},{2,0},{4,6},{6,4},{8,10},{10,8},{12,14},{14,12},{16,18},{18,... | collective-permute-start | bytes 1572872 | tf_op jit(solution)/shard_map/ppermute | solution.py:235
  296.8 28.8 %collective-permute-start.47 = (bf16[192,3072]{1,0:T(8,128)(2,1)S(1)}, bf16[192,3072]{1,0:T(8,128)(2,1)S(1)}, u32[]{:S(2)}, u32[]{:S(2)}) collective-permute-start(bf16[192,3072]{1,0:T(8,128)(2,1)S(1)} %dynamic-slice_bitcast_fusion.1), channel_id=1, source_target_pairs={{0,1},{1,0},{2,3},{3,2},{4,5},{5,4},{6,7},{7,6},{8,9},{9,8},{10,11... | collective-permute-start | bytes 3538952 | tf_op jit(solution)/shard_map/ppermute | solution.py:241
  300.3 127.2 %collective-permute-start.44 = (bf16[192,768]{1,0:T(8,128)(2,1)}, bf16[192,768]{1,0:T(8,128)(2,1)}, u32[]{:S(2)}, u32[]{:S(2)}) collective-permute-start(bf16[192,768]{1,0:T(8,128)(2,1)} %dynamic-slice_bitcast_fusion.4), channel_id=1, source_target_pairs={{0,1},{1,0},{2,3},{3,2},{4,5},{5,4},{6,7},{7,6},{8,9},{9,8},{10,11... | collective-permute-start | bytes 884744 | tf_op jit(solution)/shard_map/ppermute | solution.py:241
  302.1 29.7 %collective-permute-start.25 = (bf16[1024,128]{1,0:T(8,128)(2,1)S(1)}, bf16[1024,128]{1,0:T(8,128)(2,1)S(1)}, u32[]{:S(2)}, u32[]{:S(2)}) collective-permute-start(bf16[1024,128]{1,0:T(8,128)(2,1)S(1)} %slice.221), channel_id=1, source_target_pairs={{0,4},{2,6},{4,0},{6,2},{8,12},{10,14},{12,8},{14,10},{16,20},{18,... | collective-permute-start | bytes 786440 | tf_op jit(solution)/shard_map/ppermute | solution.py:235
  328.5 147.1 %reduce-scatter.8.cloned.1.call-start = ((), (), s32[]{:S(2)}) async-start(), calls=%async_computation.6 | async-start | bytes 1327104 | tf_op jit(solution)/shard_map/reduce_scatter | solution.py:468
  336.9 26.9 %collective-permute-start.50 = (bf16[768,768]{1,0:T(8,128)(2,1)}, bf16[768,768]{1,0:T(8,128)(2,1)}, u32[]{:S(2)}, u32[]{:S(2)}) collective-permute-start(bf16[768,768]{1,0:T(8,128)(2,1)} %dynamic-slice_bitcast_fusion), channel_id=1, source_target_pairs={{0,1},{1,0},{2,3},{3,2},{4,5},{5,4},{6,7},{7,6},{8,9},{9,8},{10,11... | collective-permute-start | bytes 3538952 | tf_op jit(solution)/shard_map/ppermute | solution.py:241
  366.3 167.7 %reduce-scatter.4.cloned.1.call-start = ((), (), s32[]{:S(2)}) async-start(), calls=%async_computation.3 | async-start | bytes 331776 | tf_op jit(solution)/shard_map/reduce_scatter | solution.py:468
  420.8 27.6 %collective-permute-start.27 = (bf16[256,576]{0,1:T(8,128)(2,1)S(1)}, bf16[256,576]{0,1:T(8,128)(2,1)S(1)}, u32[]{:S(2)}, u32[]{:S(2)}) collective-permute-start(bf16[256,576]{0,1:T(8,128)(2,1)S(1)} %get-tuple-element.126), channel_id=1, source_target_pairs={{0,16},{2,18},{4,20},{6,22},{8,24},{10,26},{12,28},{14,30},{16,0},... | collective-permute-start | bytes 884744 | tf_op jit(solution)/shard_map/ppermute | solution.py:232
  422.1 29.4 %collective-permute-start.28 = (bf16[256,576]{0,1:T(8,128)(2,1)}, bf16[256,576]{0,1:T(8,128)(2,1)S(1)}, u32[]{:S(2)}, u32[]{:S(2)}) collective-permute-start(bf16[256,576]{0,1:T(8,128)(2,1)} %get-tuple-element.125), channel_id=1, source_target_pairs={{0,8},{2,10},{4,12},{6,14},{8,16},{10,18},{12,20},{14,22},{16,24},... | collective-permute-start | bytes 884744 | tf_op jit(solution)/shard_map/ppermute | solution.py:232
  431.3 145.3 %all-gather.3.cloned.1.call-start = ((), (), s32[]{:S(2)}) async-start(), calls=%async_computation.5 | async-start | bytes 1327104 | tf_op jit(solution)/shard_map/all_gather | solution.py:471
  451.4 167.3 %all-gather.5.cloned.1.call-start = ((), (), s32[]{:S(2)}) async-start(), calls=%async_computation.7 | async-start | bytes 1327104 | tf_op jit(solution)/shard_map/all_gather | solution.py:471
  489.6 131.8 %collective-permute-start.42 = (bf16[192,4,576]{2,0,1:T(8,128)(2,1)}, bf16[192,4,576]{2,0,1:T(8,128)(2,1)}, u32[]{:S(2)}, u32[]{:S(2)}) collective-permute-start(bf16[192,4,576]{2,0,1:T(8,128)(2,1)} %maximum_select_fusion.4), channel_id=1, source_target_pairs={{0,2},{2,0},{4,6},{6,4},{8,10},{10,8},{12,14},{14,12},{16,18},{18,... | collective-permute-start | bytes 2654216 | tf_op jit(solution)/shard_map/ppermute | solution.py:235
  565.4 53.3 %collective-permute-start.45 = (bf16[192,768]{1,0:T(8,128)(2,1)S(1)}, bf16[192,768]{1,0:T(8,128)(2,1)S(1)}, u32[]{:S(2)}, u32[]{:S(2)}) collective-permute-start(bf16[192,768]{1,0:T(8,128)(2,1)S(1)} %all_gather.9), channel_id=1, source_target_pairs={{0,2},{2,0},{4,6},{6,4},{8,10},{10,8},{12,14},{14,12},{16,18},{18,... | collective-permute-start | bytes 884744 | tf_op jit(solution)/shard_map/ppermute | solution.py:235
  576.6 52.4 %collective-permute-start.48 = (bf16[192,3072]{1,0:T(8,128)(2,1)}, bf16[192,3072]{1,0:T(8,128)(2,1)}, u32[]{:S(2)}, u32[]{:S(2)}) collective-permute-start(bf16[192,3072]{1,0:T(8,128)(2,1)} %all-gather.3.cloned.1.call-done), channel_id=1, source_target_pairs={{0,2},{2,0},{4,6},{6,4},{8,10},{10,8},{12,14},{14,12},{16,18},{18,... | collective-permute-start | bytes 3538952 | tf_op jit(solution)/shard_map/ppermute | solution.py:235
  (82 other events, 1094.7 us)
Sparse Core Ops, SparseCore 0:
  328.6 61.5 reduce-scatter.5
  394.2 75.2 reduce-scatter.7
  473.4 60.6 reduce-scatter.3
  536.1 40.4 all-gather.2
  578.6 39.9 all-gather.4
